TPU v7x, 256 devices: a whole 4x4x8 slice. The times are simulated.
256 devices in a mesh: node: 64 (over y, z_hi, x, core), local: 4 (over z_lo).
Axes of the slice: x: 4, y: 4, z: 8 (z_hi: 2, z_lo: 4; z = z_hi * 4 + z_lo), core: 2. Of those that a mesh axis runs over, the one named last changes fastest.
Arguments:
- tokens: bfloat16 [65536, 4096], P(('node', 'local')), may hold values from -24 to 24
- queries: bfloat16 [65536, 4096], P(('node', 'local')), may hold values from -240 to 240
- values: bfloat16 [65536, 512], P(('node', 'local')), may hold values from -6 to 6
- upstream: bfloat16 [65536, 4096], P(('node', 'local')), may hold values from -6 to 6
- key_weight: bfloat16 [4096, 512], P(('node', 'local')), may hold values from -0.09375 to 0.09375
- positions: int32 [65536], P(('node', 'local')), may hold values from 0 to 255, as said below
Outputs:
- grad_tokens: bfloat16 [65536, 4096], P(('node', 'local'))
- grad_weight: float32 [4096, 512], P(('node', 'local'))
Inputs may be any that keep to these rules, and one draw needn't show every extreme that they name: positions[i] counts the earlier tokens of token i's document; every block of 256 rows starts a document, and no document crosses such a block.
All inputs are finite; a program needn't handle non-finite values.
Results may differ from a plain program's by a relative error of at most 0.033.
Values may be sent and summed in bfloat16 or wider, within the bound.
A program may use at most 128 MiB of HBM per device.

v0:
```python
import jax
import jax.numpy as jnp
from jax import lax
from jax.sharding import Mesh
from jax.sharding import PartitionSpec as P

HEAD_SIZE = 128
NODE = ("node_0", "node_1", "node_2", "node_3")
NODE_LOCAL = ("node_0", "node_1", "node_2", "node_3", "local")


def piece_ends(length, count):
    unit = 8 if length >= 8 * count else 1
    return [length // unit * k // count * unit for k in range(1, count)]


def stacked_from(shard, axes, sequence):
    tiles = shard
    for k in sequence:
        tiles = lax.all_gather(tiles, axes[k])
    done = sequence[::-1]
    back = [done.index(k) for k in range(len(axes))]
    tiles = tiles.transpose(*back, *range(len(axes), tiles.ndim))
    return tiles.reshape(-1, *shard.shape)


def in_order(tiles, dim):
    tiles = jnp.moveaxis(tiles, 0, dim)
    dims = tiles.shape
    return tiles.reshape(*dims[:dim], dims[dim] * dims[dim + 1], *dims[dim + 2 :])


def gather_at_once(shard, axes, dim):
    numbers = list(range(len(axes)))[::-1]
    widest = shard.shape.index(max(shard.shape[:-1] or shard.shape))
    edges = [0, *piece_ends(shard.shape[widest], len(axes)), shard.shape[widest]]
    outs = []
    for k, (start, end) in enumerate(zip(edges, edges[1:])):
        if end > start:
            section = lax.slice_in_dim(shard, start, end, axis=widest)
            outs.append(stacked_from(section, axes, numbers[k:] + numbers[:k]))
    return in_order(jnp.concatenate(outs, axis=widest + 1), dim)


def cut_along(shard, dim, size):
    dims = shard.shape
    tiles = shard.reshape(*dims[:dim], size, dims[dim] // size, *dims[dim + 1 :])
    return jnp.moveaxis(tiles, dim, 0)


def sent_and_summed(shard, axis, dim):
    tiles = cut_along(shard, dim, lax.axis_size(axis))
    arrived = lax.all_to_all(tiles, axis, split_axis=0, concat_axis=0, tiled=True)
    return arrived.sum(axis=0)


def angle_tables(positions, head_width):
    half = head_width // 2
    freq = jnp.exp(
        -(jnp.arange(half, dtype=jnp.float32) * 2.0 / head_width) * jnp.log(jnp.float32(1000000.0))
    )
    angle = positions.astype(jnp.float32)[:, None] * freq[None, :]
    return (jnp.cos(angle)[:, None, :], jnp.sin(angle)[:, None, :])


def rotate(raw_keys, cosine, sine_part, head_width, sign):
    item_count, width = raw_keys.shape
    shaped = raw_keys.reshape(item_count, width // head_width, head_width)
    half = head_width // 2
    first, second = (shaped[..., :half], shaped[..., half:])
    joined = jnp.concatenate(
        [first * cosine - sign * second * sine_part, second * cosine + sign * first * sine_part],
        axis=-1,
    )
    return joined.reshape(item_count, width)


def attend_back(queries, keys, values, upstream, positions, head_width):
    item_count, width = keys.shape
    key_value_count = width // head_width
    group_size = queries.shape[1] // width
    scale = head_width ** (-0.5)
    qmat = queries.reshape(item_count, key_value_count, group_size, head_width)
    kmat = keys.reshape(item_count, key_value_count, head_width)
    value_matrix = values.reshape(item_count, key_value_count, head_width)
    upper_matrix = upstream.reshape(item_count, key_value_count, group_size, head_width)
    scores = jnp.einsum("yxru,oxu->xryo", qmat, kmat, preferred_element_type=jnp.float32) * scale
    place = jnp.arange(item_count, dtype=jnp.int32)
    allowed = (place[None, :] <= place[:, None]) & (place[None, :] >= (place - positions)[:, None])
    scores = jnp.where(allowed, scores, jnp.float32(-1e30))
    top = jnp.max(scores, axis=-1, keepdims=True)
    expo = jnp.exp(scores - top)
    probs = expo / jnp.sum(expo, axis=-1, keepdims=True)
    slope_values = jnp.einsum(
        "yxru,oxu->xryo", upper_matrix, value_matrix, preferred_element_type=jnp.float32
    )
    inner = jnp.sum(probs * slope_values, axis=-1, keepdims=True)
    dscores = (probs * (slope_values - inner) * scale).astype(jnp.bfloat16)
    grad_rot = jnp.einsum("kgts,tkgd->skd", dscores, qmat, preferred_element_type=jnp.float32)
    return grad_rot.reshape(item_count, width)


def per_device(tokens, queries, values, upstream, key_weight, positions):
    node_count = lax.axis_size(NODE)
    local_count = lax.axis_size("local")
    local_index = lax.axis_index("local")
    shard_rows = key_weight.shape[0]
    key_width = key_weight.shape[1]
    item_count = tokens.shape[0]
    model_width = tokens.shape[1]
    head_width = HEAD_SIZE
    whole_weight = gather_at_once(key_weight, NODE_LOCAL, 0)
    raw_keys = jnp.dot(tokens, whole_weight, preferred_element_type=jnp.float32)
    grouped = whole_weight.reshape(node_count, local_count, shard_rows, key_width)
    quarter = lax.dynamic_index_in_dim(grouped, local_index, 1, keepdims=False)
    quarter = quarter.reshape(node_count * shard_rows, key_width)
    cosine, sine_part = angle_tables(positions, head_width)
    keys = rotate(raw_keys, cosine, sine_part, head_width, 1.0).astype(jnp.bfloat16)
    grad_rot = attend_back(queries, keys, values, upstream, positions, head_width)
    grad_keys = rotate(grad_rot, cosine, sine_part, head_width, -1.0).astype(jnp.bfloat16)
    mixed = lax.dot_general(
        grad_keys,
        lax.all_gather(quarter, "local", axis=0, tiled=True),
        (((1,), (1,)), ((), ())),
        preferred_element_type=jnp.float32,
    ).astype(jnp.bfloat16)
    grad_tokens = mixed.reshape(item_count, local_count, node_count, shard_rows)
    grad_tokens = jnp.transpose(grad_tokens, (0, 2, 1, 3)).reshape(item_count, model_width)
    sectioned = lax.psum_scatter(
        lax.dot_general(
            tokens, grad_keys, (((0,), (0,)), ((), ())), preferred_element_type=jnp.float32
        ),
        NODE,
        scatter_dimension=0,
        tiled=True,
    )
    grad_weight = sent_and_summed(sectioned, "local", 0)
    return (grad_tokens, grad_weight)


def solution(mesh):
    torus = Mesh(
        mesh.devices.reshape(4, 2, 4, 2, mesh.shape["local"]),
        ("node_0", "node_1", "node_2", "node_3", "local"),
    )
    placed = (
        P(NODE_LOCAL, None),
        P(NODE_LOCAL, None),
        P(NODE_LOCAL, None),
        P(NODE_LOCAL, None),
        P(NODE_LOCAL, None),
        P(NODE_LOCAL),
    )
    return jax.shard_map(
        per_device,
        mesh=torus,
        in_specs=placed,
        out_specs=(P(NODE_LOCAL, None), P(NODE_LOCAL, None)),
        check_vma=False,
    )
```

profile of v0, /device:TPU:2, one launch (start us, length us, event | category | flops | bytes accessed | tf_op | source)
XLA Modules:
  0.0 925.6 jit_solution(6340969713008578064)
XLA Ops:
  8.1 12.4 %all-gather.29 = bf16[4,4,512]{2,1,0:T(4,128)(2,1)S(1)} all-gather(bf16[1,4,512]{2,1,0:T(4,128)(2,1)S(1)} %slice_bitcast_fusion), channel_id=22, replica_groups=mesh['node_0'=4,'node_1'=2,'node_2'=4,'node_3'=2,'local'=4] {'node_0'}, dimensions={0}, use_global_device_ids=true | all-gather | bytes 20480 | tf_op jit(solution)/shard_map/all_gather | solution.py:20
  20.5 14.0 %all-gather.21 = bf16[16,4,512]{2,1,0:T(4,128)(2,1)S(1)} all-gather(bf16[4,4,512]{2,1,0:T(4,128)(2,1)S(1)} %all-gather.29), channel_id=23, replica_groups=mesh['node_0'=4,'node_1'=2,'node_2'=4,'node_3'=2,'local'=4] {'local'}, dimensions={0}, use_global_device_ids=true | all-gather | bytes 81920 | tf_op jit(solution)/shard_map/all_gather | solution.py:20
  36.4 13.9 %all-gather.23 = bf16[8,4,4,4,512]{4,3,2,1,0:T(4,128)(2,1)} all-gather(bf16[2,4,4,4,512]{4,3,2,1,0:T(4,128)(2,1)S(1)} %bitcast.150), channel_id=25, replica_groups=mesh['node_0'=4,'node_1'=2,'node_2'=4,'node_3'=2,'local'=4] {'node_2'}, dimensions={0}, use_global_device_ids=true | all-gather | bytes 655360 | tf_op jit(solution)/shard_map/all_gather | solution.py:20
  53.0 11.9 %all-gather.6 = bf16[8,3,512]{2,1,0:T(4,128)(2,1)S(1)} all-gather(bf16[2,3,512]{2,1,0:T(4,128)(2,1)S(1)} %all-gather.26), channel_id=8, replica_groups=mesh['node_0'=4,'node_1'=2,'node_2'=4,'node_3'=2,'local'=4] {'node_2'}, dimensions={0}, use_global_device_ids=true | all-gather | bytes 30720 | tf_op jit(solution)/shard_map/all_gather | solution.py:20
  64.9 10.9 %all-gather.7 = bf16[8,2,3,512]{3,1,2,0:T(2,128)(2,1)S(1)} all-gather(bf16[4,2,3,512]{3,1,2,0:T(2,128)(2,1)S(1)} %copy.135), channel_id=9, replica_groups=mesh['node_0'=4,'node_1'=2,'node_2'=4,'node_3'=2,'local'=4] {'node_1'}, dimensions={0}, use_global_device_ids=true | all-gather | bytes 73728 | tf_op jit(solution)/shard_map/all_gather | solution.py:20
  75.8 12.1 %all-gather.8 = bf16[8,4,2,3,512]{4,1,3,2,0:T(4,128)(2,1)S(1)} all-gather(bf16[2,4,2,3,512]{4,1,3,2,0:T(4,128)(2,1)S(1)} %copy.136), channel_id=10, replica_groups=mesh['node_0'=4,'node_1'=2,'node_2'=4,'node_3'=2,'local'=4] {'node_0'}, dimensions={0}, use_global_device_ids=true | all-gather | bytes 245760 | tf_op jit(solution)/shard_map/all_gather | solution.py:20
  87.9 20.1 %all-gather.9 = bf16[16,2,4,2,3,512]{5,2,4,3,1,0:T(4,128)(2,1)S(1)} all-gather(bf16[4,2,4,2,3,512]{5,2,4,3,1,0:T(4,128)(2,1)S(1)} %bitcast.149), channel_id=11, replica_groups=mesh['node_0'=4,'node_1'=2,'node_2'=4,'node_3'=2,'local'=4] {'local'}, dimensions={0}, use_global_device_ids=true | all-gather | bytes 983040 | tf_op jit(solution)/shard_map/all_gather | solution.py:20
  109.4 12.0 %all-gather.27 = bf16[4,3,512]{2,1,0:T(4,128)(2,1)S(1)} all-gather(bf16[1,3,512]{2,1,0:T(4,128)(2,1)S(1)} %get-tuple-element.19), channel_id=12, replica_groups=mesh['node_0'=4,'node_1'=2,'node_2'=4,'node_3'=2,'local'=4] {'node_2'}, dimensions={0}, use_global_device_ids=true | all-gather | bytes 15360 | tf_op jit(solution)/shard_map/all_gather | solution.py:20
  121.3 8.3 all-gather.11
  129.6 11.9 %all-gather.12 = bf16[8,4,3,512]{3,1,2,0:T(4,128)(2,1)S(1)} all-gather(bf16[2,4,3,512]{3,1,2,0:T(4,128)(2,1)S(1)} %copy.139), channel_id=14, replica_groups=mesh['node_0'=4,'node_1'=2,'node_2'=4,'node_3'=2,'local'=4] {'node_0'}, dimensions={0}, use_global_device_ids=true | all-gather | bytes 122880 | tf_op jit(solution)/shard_map/all_gather | solution.py:20
  141.6 14.2 %all-gather.13 = bf16[16,2,4,3,512]{4,2,3,1,0:T(4,128)(2,1)S(1)} all-gather(bf16[4,2,4,3,512]{4,2,3,1,0:T(4,128)(2,1)S(1)} %bitcast.154), channel_id=15, replica_groups=mesh['node_0'=4,'node_1'=2,'node_2'=4,'node_3'=2,'local'=4] {'local'}, dimensions={0}, use_global_device_ids=true | all-gather | bytes 491520 | tf_op jit(solution)/shard_map/all_gather | solution.py:20
  159.8 8.3 all-gather.28
  168.0 11.9 %all-gather.16 = bf16[8,3,512]{2,1,0:T(4,128)(2,1)S(1)} all-gather(bf16[2,3,512]{2,1,0:T(4,128)(2,1)S(1)} %all-gather.28), channel_id=18, replica_groups=mesh['node_0'=4,'node_1'=2,'node_2'=4,'node_3'=2,'local'=4] {'node_0'}, dimensions={0}, use_global_device_ids=true | all-gather | bytes 30720 | tf_op jit(solution)/shard_map/all_gather | solution.py:20
  180.0 13.2 %all-gather.17 = bf16[16,2,3,512]{3,1,2,0:T(2,128)(2,1)S(1)} all-gather(bf16[4,2,3,512]{3,1,2,0:T(2,128)(2,1)S(1)} %copy.141), channel_id=19, replica_groups=mesh['node_0'=4,'node_1'=2,'node_2'=4,'node_3'=2,'local'=4] {'local'}, dimensions={0}, use_global_device_ids=true | all-gather | bytes 122880 | tf_op jit(solution)/shard_map/all_gather | solution.py:20
  195.2 14.5 %all-gather.19 = bf16[8,4,4,2,3,512]{5,2,4,3,1,0:T(4,128)(2,1)S(1)} all-gather(bf16[2,4,4,2,3,512]{5,2,4,3,1,0:T(4,128)(2,1)S(1)} %bitcast.147), channel_id=21, replica_groups=mesh['node_0'=4,'node_1'=2,'node_2'=4,'node_3'=2,'local'=4] {'node_2'}, dimensions={0}, use_global_device_ids=true | all-gather | bytes 983040 | tf_op jit(solution)/shard_map/all_gather | solution.py:20
  212.2 13.1 %all-gather.25 = bf16[4,3,512]{2,1,0:T(4,128)(2,1)S(1)} all-gather(bf16[1,3,512]{2,1,0:T(4,128)(2,1)S(1)} %get-tuple-element.21), channel_id=2, replica_groups=mesh['node_0'=4,'node_1'=2,'node_2'=4,'node_3'=2,'local'=4] {'local'}, dimensions={0}, use_global_device_ids=true | all-gather | bytes 15360 | tf_op jit(solution)/shard_map/all_gather | solution.py:20
  227.1 11.9 %all-gather.2 = bf16[8,4,3,512]{3,1,2,0:T(4,128)(2,1)S(1)} all-gather(bf16[2,4,3,512]{3,1,2,0:T(4,128)(2,1)S(1)} %copy.133), channel_id=4, replica_groups=mesh['node_0'=4,'node_1'=2,'node_2'=4,'node_3'=2,'local'=4] {'node_2'}, dimensions={0}, use_global_device_ids=true | all-gather | bytes 122880 | tf_op jit(solution)/shard_map/all_gather | solution.py:20
  239.0 10.2 %all-gather.3 = bf16[8,2,4,3,512]{4,2,3,1,0:T(4,128)(2,1)S(1)} all-gather(bf16[4,2,4,3,512]{4,2,3,1,0:T(4,128)(2,1)S(1)} %bitcast.153), channel_id=5, replica_groups=mesh['node_0'=4,'node_1'=2,'node_2'=4,'node_3'=2,'local'=4] {'node_1'}, dimensions={0}, use_global_device_ids=true | all-gather | bytes 294912 | tf_op jit(solution)/shard_map/all_gather | solution.py:20
  249.3 14.1 %all-gather.4 = bf16[8,4,2,4,3,512]{5,3,4,2,1,0:T(4,128)(2,1)S(1)} all-gather(bf16[2,4,2,4,3,512]{5,3,4,2,1,0:T(4,128)(2,1)S(1)} %bitcast.148), channel_id=6, replica_groups=mesh['node_0'=4,'node_1'=2,'node_2'=4,'node_3'=2,'local'=4] {'node_0'}, dimensions={0}, use_global_device_ids=true | all-gather | bytes 983040 | tf_op jit(solution)/shard_map/all_gather | solution.py:20
  265.1 4.1 copy.190
  275.6 6.2 fusion.15
  284.5 53.9 %concatenate.24 = bf16[256,16,512]{2,1,0:T(8,128)(2,1)} concatenate(bf16[256,3,512]{2,1,0:T(4,128)(2,1)} %bitcast.121, bf16[256,3,512]{2,1,0:T(4,128)(2,1)S(1)} %bitcast.119, bf16[256,3,512]{2,1,0:T(4,128)(2,1)} %bitcast.133, bf16[256,3,512]{2,1,0:T(4,128)(2,1)} %bitcast.134, bf16[256,4,512]{2,1,0:T(4,128)(2,1)} %bitcast.123), dimensions={1} | concatenate | bytes 8388608 | tf_op jit(solution)/shard_map/concatenate | solution.py:42
  347.0 6.1 fusion.20
  353.1 12.9 %fusion.13 = f32[4,8,256,256]{2,3,1,0:T(8,128)} fusion(f32[4,256,256,8]{2,1,3,0:T(8,128)} %fusion.20, pred[256,256]{0,1:T(8,128)(4,1)} %fusion.24), kind=kOutput, calls=%fused_computation.18 | output fusion | flops 12599806 | bytes 16842752 | tf_op jit(solution)/shard_map/div | solution.py:93
  366.0 14.2 %fusion.17 = f32[256,4,128]{2,0,1:T(8,128)} fusion(bf16[256,4,8,128]{0,3,2,1:T(8,128)(2,1)} %bitcast.128, f32[4,8,256,256]{2,3,1,0:T(8,128)} %fusion.13, f32[4,256,256,8]{2,1,3,0:T(8,128)} %fusion.15), kind=kOutput, calls=%fused_computation.22 | convolution fusion | flops 547365120 | bytes 19398656 | tf_op jit(solution)/shard_map/kgts,tkgd->skd/dot_general | solution.py:99
  383.7 4.5 convolution_bitcast_fusion
  388.2 9.0 copy.183
  404.0 53.9 %concatenate.32 = bf16[64,4,16,512]{3,2,1,0:T(8,128)(2,1)} concatenate(bf16[64,4,3,512]{3,2,1,0:T(4,128)(2,1)} %bitcast.122, bf16[64,4,3,512]{3,2,1,0:T(4,128)(2,1)S(1)} %bitcast.120, bf16[64,4,3,512]{3,2,1,0:T(4,128)(2,1)} %copy.164, bf16[64,4,3,512]{3,2,1,0:T(4,128)(2,1)} %copy.165, bf16[64,4,4,512]{3,2,1,0:T(4,128)(2,1)} %bitcast.124), dimensions={2} | concatenate | bytes 8388608 | tf_op jit(solution)/shard_map/concatenate | solution.py:42
  460.1 352.6 %reduce-scatter.4.cloned.1.call-done = f32[64,512]{1,0:T(8,128)} async-done(((f32[4096,512]{1,0:T(8,128)}), f32[64,512]{1,0:T(8,128)}) %reduce-scatter.4.cloned.1.call-update) | async-done | bytes 131088 | tf_op jit(solution)/shard_map/reduce_scatter | solution.py:129
  816.1 86.2 %all-gather.33.cloned.1.call-done = bf16[4096,512]{1,0:T(8,128)(2,1)} async-done(((bf16[1024,512]{1,0:T(8,128)(2,1)}), bf16[4096,512]{1,0:T(8,128)(2,1)}) %all-gather.33.cloned.1.call-update) | async-done | bytes 4194320 | tf_op jit(solution)/shard_map/all_gather | solution.py:123
  902.3 4.8 convolution_convert_fusion
  907.1 4.1 copy.166
  (58 shorter events, 60.3 us)
Async XLA Ops:
  7.2 331.2 %copy-start = (bf16[256,4096]{1,0:T(8,128)(2,1)S(1)}, bf16[256,4096]{1,0:T(8,128)(2,1)}, u32[]{:S(2)}) copy-start(bf16[256,4096]{1,0:T(8,128)(2,1)} %param.6) | copy-start | bytes 6291460
  7.2 274.6 %all-gather.35.cloned.1.call-start = ((), (), s32[]{:S(2)}) async-start(), calls=%async_computation.3 | async-start | bytes 1572864 | tf_op jit(solution)/shard_map/all_gather | solution.py:20
  50.3 762.5 %reduce-scatter.4.cloned.1.call-start = ((), (), s32[]{:S(2)}) async-start(), calls=%async_computation.4 | async-start | bytes 8519680 | tf_op jit(solution)/shard_map/reduce_scatter | solution.py:129
  158.1 106.9 %copy-start.1 = (bf16[8,4,2,4,3,512]{5,3,4,2,1,0:T(4,128)(2,1)}, bf16[8,4,2,4,3,512]{5,3,4,2,1,0:T(4,128)(2,1)S(1)}, u32[]{:S(2)}) copy-start(bf16[8,4,2,4,3,512]{5,3,4,2,1,0:T(4,128)(2,1)S(1)} %all-gather.14) | copy-start | bytes 2359300
  158.2 106.9 %copy-start.3 = (s32[256]{0:T(256)S(1)}, s32[256]{0:T(256)}, u32[]{:S(2)}) copy-start(s32[256]{0:T(256)} %param.11) | copy-start | bytes 3076
  209.7 0.9 copy-start.2
  397.2 505.0 %all-gather.33.cloned.1.call-start = ((), (), s32[]{:S(2)}) async-start(), calls=%async_computation.2 | async-start | bytes 5242880 | tf_op jit(solution)/shard_map/all_gather | solution.py:123
  812.7 105.7 %all-to-all-start = ((f32[4,16,512]{2,1,0:T(8,128)}), f32[4,16,512]{2,1,0:T(8,128)S(1)}, u32[]{:S(2)}, u32[]{:S(2)}) async-start(f32[4,16,512]{2,1,0:T(8,128)} %bitcast.161), calls=%async_computation | async-start | bytes 262144 | tf_op jit(solution)/shard_map/all_to_all | solution.py:53
Sparse Core Ops, SparseCore 0:
  50.4 37.0 all-gather.34
  397.4 415.3 reduce-scatter.3
  815.1 87.1 all-gather.32
where the time goes:
time: 934 us; the launch traced here: 926 us
  waiting for transfers between devices  439 us (47%)
  blocking collectives  249 us (27%)
  local copies, waits for them, and re-layouts  162 us (17%)
  matrix products  39.3 us (4%)
  other arithmetic  19.2 us (2%)
  between operations  13.9 us (1%)
    reduce_scatter x1, waiting for transfers between devices, per_device(): lax.psum_scatter(lax.dot_general(tokens, grad_keys, (((0,), (0,)), ((), (...  353 us
    all_gather x24, blocking collectives, stacked_from(): tiles = lax.all_gather(tiles, axes[k])  249 us
    concatenate x4, local copies, waits for them, and re-layouts, gather_at_once(): return in_order(jnp.concatenate(outs, axis=widest + 1), dim)  111 us
    all_gather x1, waiting for transfers between devices, per_device(): lax.all_gather(quarter, 'local', axis=0, tiled=True)  86.2 us
    unnamed x15, local copies, waits for them, and re-layouts  22.1 us
  transfers between devices with their start and end apart: 4, of which 2 were waited for; matrix products, arithmetic and copies ran while one was open for 11% of the time, Pallas kernels for 0%

commit v1 on v0

v1 whole, which is shorter than its diff:
```python
import math

import jax
import jax.numpy as jnp
from jax import lax
from jax.experimental import pallas as pl
from jax.experimental.pallas import tpu as pltpu
from jax.sharding import Mesh
from jax.sharding import PartitionSpec as P

AXES = ("y", "zh", "x", "c", "zl")
MESH = pl.DeviceIdType.MESH
HEADS = 4
GROUP = 8
HEAD = 128
TOK = 256
D = 4096
SCALE = HEAD**-0.5
BF = jnp.bfloat16
F32 = jnp.float32
NT = (((1,), (1,)), ((), ()))


def dot_nt(a, b):
    return lax.dot_general(a, b, NT, preferred_element_type=F32)


def dot(a, b):
    return jnp.dot(a, b, preferred_element_type=F32)


def kernel(
    tok_hbm, q_hbm, v_hbm, u_hbm, kw_hbm, pos_hbm,
    gt_hbm, gw_out,
    tok, q, v, u, kw, pos, W, TT, cosine, sine, bias, keys, acc, gk, gt,
    own, other, RC, A, RAE, RAO, B, RB, C, RZ,
    load_sem, store_sem,
    zs, zr, s1s, s1r, s2s, s2r, cs, cr,
    rcs, rcr, ras, rar, rbs, rbr, rzs, rzr,
):
    y, zh, x, c, zl = (lax.axis_index(a) for a in AXES)
    z = zh * 4 + zl
    other_core = (y, zh, x, 1 - c, zl)

    def at_x(k):
        return (y, zh, lax.rem(x + k, 4), c, zl)

    def at_y(k):
        return (lax.rem(y + k, 4), zh, x, c, zl)

    def at_z(k):
        there = lax.rem(z + k, 8)
        return (y, there // 4, x, c, lax.rem(there, 4))

    def send(src, dst, send_sem, recv_sem, where):
        pltpu.make_async_remote_copy(
            src_ref=src, dst_ref=dst, send_sem=send_sem, recv_sem=recv_sem,
            device_id=where, device_id_type=MESH,
        ).start()

    def wait(like, sem):
        pltpu.make_async_copy(like, like, sem).wait()

    loads = [(kw_hbm, kw), (pos_hbm, pos), (tok_hbm, tok), (v_hbm, v), (q_hbm, q), (u_hbm, u)]
    copies = [pltpu.make_async_copy(a, b, load_sem.at[i]) for i, (a, b) in enumerate(loads)]
    for copy in copies:
        copy.start()
    barrier = pltpu.get_barrier_semaphore()
    peers = [other_core] + [at_x(k) for k in (1, 2, 3)] + [at_y(k) for k in (1, 2, 3)]
    peers += [at_z(k) for k in range(1, 8)]
    for peer in peers:
        pl.semaphore_signal(barrier, inc=1, device_id=peer, device_id_type=MESH)
    copies[0].wait()
    for h in range(HEADS):
        W[h, y, zh, x, c, zl] = kw[:, h * HEAD : (h + 1) * HEAD]
    pl.semaphore_wait(barrier, len(peers))

    mine = W.at[:, y, zh, x, c, zl]
    for k in range(1, 8):
        send(mine, mine, zs.at[k - 1], zr.at[k - 1], at_z(k))

    copies[1].wait()
    lane = lax.broadcasted_iota(jnp.int32, (1, HEAD), 1)
    half = HEAD // 2
    freq = jnp.exp(-(lax.rem(lane, half).astype(F32) * 2.0 / HEAD) * math.log(1000000.0))
    place = pos[...].astype(F32)
    column = jnp.broadcast_to(place, (HEAD, TOK)).T
    angle = column * freq
    cosine[...] = jnp.cos(angle)
    sine[...] = jnp.where(lane < half, -1.0, 1.0) * jnp.sin(angle)
    row = lax.broadcasted_iota(jnp.int32, (TOK, TOK), 0)
    col = lax.broadcasted_iota(jnp.int32, (TOK, TOK), 1)
    allowed = (row <= col) & (row >= col - pos[...])
    bias[...] = jnp.where(allowed, 0.0, -1e30).astype(F32)

    copies[2].wait()

    def turn(i, _):
        block = tok[:, pl.ds(pl.multiple_of(i * HEAD, HEAD), HEAD)].T
        TT[c, i] = block[:64]
        TT[1 - c, i] = block[64:]
        return 0

    lax.fori_loop(0, 32, turn, 0)

    for k in range(1, 8):
        wait(mine, zr.at[k - 1])

    def first_slice(h):
        return W.at[h, y, :, x, c]

    def second_slice(h):
        return W.at[h, y, :, :, c] if h % 2 == 0 else W.at[h, :, :, x, c]

    def core_slice(h):
        return W.at[h, :, :, :, c]

    for h in range(HEADS):
        for k in (1, 2, 3):
            piece = first_slice(h)
            send(piece, piece, s1s.at[h, k - 1], s1r.at[h, k - 1], at_x(k) if h % 2 == 0 else at_y(k))
    for copy in copies[3:]:
        copy.wait()
    for h in range(HEADS):
        for k in (1, 2, 3):
            wait(first_slice(h), s1r.at[h, k - 1])
        for k in (1, 2, 3):
            piece = second_slice(h)
            send(piece, piece, s2s.at[h, k - 1], s2r.at[h, k - 1], at_y(k) if h % 2 == 0 else at_x(k))

    def to_core(h):
        for k in (1, 2, 3):
            wait(second_slice(h), s2r.at[h, k - 1])
        send(core_slice(h), core_slice(h), cs.at[h], cr.at[h], other_core)

    def r0(h):
        send(other.at[h], RC.at[h], rcs.at[h], rcr.at[h], other_core)

    def a_slice(h, k):
        if h % 2 == 0:
            return A.at[h, lax.rem(y + k, 4)]
        return A.at[h, :, :, lax.rem(x + k, 4)]

    def b_slice(h, k):
        if h % 2 == 0:
            return B.at[h, :, lax.rem(x + k, 4)]
        return B.at[h, :, lax.rem(y + k, 4)]

    def ra_slot(h, k):
        return (RAO if h % 2 else RAE).at[h // 2, k - 1]

    def r1(h):
        wait(RC.at[h], rcr.at[h])

        def add(i, _):
            A[h, i] = (own[h, i] + RC[h, i].astype(F32)).astype(BF)
            return 0

        lax.fori_loop(0, 4, add, 0)
        for k in (1, 2, 3):
            send(a_slice(h, k), ra_slot(h, k), ras.at[h, k - 1], rar.at[h, k - 1], at_y(k) if h % 2 == 0 else at_x(k))

    def r2(h):
        for k in (1, 2, 3):
            wait(ra_slot(h, k), rar.at[h, k - 1])
        for i in range(2):
            for j in range(4):
                if h % 2 == 0:
                    total = A[h, y, i, j].astype(F32)
                    for k in range(3):
                        total = total + RAE[h // 2, k, i, j].astype(F32)
                else:
                    total = A[h, j, i, x].astype(F32)
                    for k in range(3):
                        total = total + RAO[h // 2, k, j, i].astype(F32)
                B[h, i, j] = total
        for k in (1, 2, 3):
            send(b_slice(h, k), RB.at[h, k - 1], rbs.at[h, k - 1], rbr.at[h, k - 1], at_x(k) if h % 2 == 0 else at_y(k))

    def r3(h):
        for k in (1, 2, 3):
            wait(RB.at[h, k - 1], rbr.at[h, k - 1])
        me = x if h % 2 == 0 else y
        for i in range(2):
            total = B[h, i, me]
            for k in range(3):
                total = total + RB[h, k, i]
            C[h, i] = total.reshape(4, 16, HEAD)
        for k in range(1, 8):
            there = lax.rem(z + k, 8)
            send(C.at[h, there // 4, lax.rem(there, 4)], RZ.at[h, k - 1], rzs.at[h, k - 1], rzr.at[h, k - 1], at_z(k))

    def r4(h):
        for k in range(1, 8):
            wait(RZ.at[h, k - 1], rzr.at[h, k - 1])
        total = C[h, zh, zl]
        for k in range(7):
            total = total + RZ[h, k]
        gw_out[:, h * HEAD : (h + 1) * HEAD] = total

    def project(h):
        wait(core_slice(h), cr.at[h])
        total = jnp.zeros((TOK, HEAD), F32)
        for i in range(4):
            total = total + dot(tok[:, i * 1024 : (i + 1) * 1024], W[h, i].reshape(1024, HEAD))
        keys[...] = (total * cosine[...] + pltpu.roll(total, half, 1) * sine[...]).astype(BF)

    def attend(h):
        acc[...] = jnp.zeros_like(acc)

        def one(g, _):
            lanes = pl.ds(pl.multiple_of((h * GROUP + g) * HEAD, HEAD), HEAD)
            queries = q[:, lanes]
            upper = u[:, lanes]
            scores = dot_nt(keys[...], queries)
            slopes = dot_nt(v[:, h * HEAD : (h + 1) * HEAD], upper)
            parts = []
            for b in range(2):
                n = (b + 1) * 128
                span = slice(b * 128, (b + 1) * 128)
                s = scores[:n, span] + bias[:n, span]
                top = jnp.max(s, axis=0, keepdims=True)
                expo = jnp.exp((s - top) * SCALE)
                sl = slopes[:n, span]
                norm = 1.0 / jnp.sum(expo, axis=0, keepdims=True)
                inner = jnp.sum(expo * sl, axis=0, keepdims=True) * norm
                parts.append((expo * (sl - inner) * (norm * SCALE)).astype(BF))
            low = jnp.concatenate([parts[0], jnp.zeros((128, 128), BF)], axis=0)
            dscores = jnp.concatenate([low, parts[1]], axis=1)
            acc[...] += dot(dscores, queries)
            return 0

        lax.fori_loop(0, GROUP, one, 0)

    def weight(h):
        total = acc[...]
        mine = (total * cosine[...] - pltpu.roll(total, half, 1) * sine[...]).astype(BF)
        gk[:, h * HEAD : (h + 1) * HEAD] = mine

        def give(i, _):
            eight = pl.ds(pl.multiple_of(i * 8, 8), 8)
            given = dot(TT[1, eight].reshape(512, TOK), mine)
            other[h, i] = given.astype(BF).reshape(2, 4, 64, HEAD)
            return 0

        lax.fori_loop(0, 4, give, 0)
        r0(h)

        def keep(i, _):
            eight = pl.ds(pl.multiple_of(i * 8, 8), 8)
            own[h, i] = dot(TT[0, eight].reshape(512, TOK), mine).reshape(2, 4, 64, HEAD)
            return 0

        lax.fori_loop(0, 4, keep, 0)

    def tokens_part(i):
        def one(n, _):
            rows = [W[h, n // 2, n % 2].reshape(512, HEAD) for h in range(HEADS)]
            cols = pl.ds(pl.multiple_of(n * 512, 512), 512)
            gt[:, cols] = dot_nt(gk[...], jnp.concatenate(rows, axis=1)).astype(BF)
            return 0

        lax.fori_loop(2 * i, 2 * i + 2, one, 0)
        cols = pl.ds(i * 1024, 1024)
        pltpu.make_async_copy(gt.at[:, cols], gt_hbm.at[:, cols], store_sem.at[i]).start()

    to_core(0)
    to_core(1)
    for h in range(HEADS):
        project(h)
        if h + 2 < HEADS:
            to_core(h + 2)
        attend(h)
        if h >= 1:
            r1(h - 1)
        weight(h)
        if h >= 2:
            r2(h - 2)
        if h >= 3:
            r3(h - 3)
    tokens_part(0)
    r1(3)
    r2(2)
    r3(1)
    tokens_part(1)
    tokens_part(2)
    r2(3)
    r3(2)
    r4(0)
    r4(1)
    tokens_part(3)
    r3(3)
    r4(2)
    r4(3)

    for k in range(7):
        wait(mine, zs.at[k])
    for h in range(HEADS):
        for k in range(3):
            wait(first_slice(h), s1s.at[h, k])
            wait(second_slice(h), s2s.at[h, k])
            wait(ra_slot(h, k + 1), ras.at[h, k])
            wait(RB.at[h, k], rbs.at[h, k])
        wait(core_slice(h), cs.at[h])
        wait(RC.at[h], rcs.at[h])
        for k in range(7):
            wait(RZ.at[h, k], rzs.at[h, k])
    for i in range(4):
        cols = pl.ds(i * 1024, 1024)
        wait(gt_hbm.at[:, cols], store_sem.at[i])


def per_device(tokens, queries, values, upstream, key_weight, positions):
    anywhere = pl.BlockSpec(memory_space=pl.ANY)
    dma = pltpu.SemaphoreType.DMA
    vm = pltpu.VMEM
    return pl.pallas_call(
        kernel,
        out_shape=(jax.ShapeDtypeStruct((TOK, D), BF), jax.ShapeDtypeStruct((16, HEADS * HEAD), F32)),
        in_specs=[anywhere] * 6,
        out_specs=(anywhere, pl.BlockSpec(memory_space=pltpu.VMEM)),
        scratch_shapes=[
            vm((TOK, D), BF), vm((TOK, D), BF), vm((TOK, HEADS * HEAD), BF), vm((TOK, D), BF),
            vm((16, HEADS * HEAD), BF), vm((1, TOK), jnp.int32),
            vm((HEADS, 4, 2, 4, 2, 4, 16, HEAD), BF),
            vm((2, 32, 64, TOK), BF),
            vm((TOK, HEAD), F32), vm((TOK, HEAD), F32), vm((TOK, TOK), F32),
            vm((TOK, HEAD), BF), vm((TOK, HEAD), F32), vm((TOK, HEADS * HEAD), BF), vm((TOK, D), BF),
            vm((HEADS, 4, 2, 4, 64, HEAD), F32),
            vm((HEADS, 4, 2, 4, 64, HEAD), BF),
            vm((HEADS, 4, 2, 4, 64, HEAD), BF),
            vm((HEADS, 4, 2, 4, 64, HEAD), BF),
            vm((2, 3, 2, 4, 64, HEAD), BF), vm((2, 3, 4, 2, 64, HEAD), BF),
            vm((HEADS, 2, 4, 64, HEAD), F32),
            vm((HEADS, 3, 2, 64, HEAD), F32),
            vm((HEADS, 2, 4, 16, HEAD), F32),
            vm((HEADS, 7, 16, HEAD), F32),
            dma((6,)), dma((4,)),
            dma((7,)), dma((7,)), dma((HEADS, 3)), dma((HEADS, 3)), dma((HEADS, 3)), dma((HEADS, 3)),
            dma((HEADS,)), dma((HEADS,)),
            dma((HEADS,)), dma((HEADS,)), dma((HEADS, 3)), dma((HEADS, 3)), dma((HEADS, 3)), dma((HEADS, 3)),
            dma((HEADS, 7)), dma((HEADS, 7)),
        ],
        compiler_params=pltpu.CompilerParams(
            collective_id=0, has_side_effects=True, vmem_limit_bytes=56 << 20
        ),
        cost_estimate=pl.CostEstimate(
            flops=5_000_000_000, bytes_accessed=9_000_000, transcendentals=2_000_000
        ),
        name="key_backward",
    )(tokens, queries, values, upstream, key_weight, positions.reshape(1, TOK))


def solution(mesh):
    torus = Mesh(mesh.devices.reshape(4, 2, 4, 2, mesh.shape["local"]), AXES)
    rows = P(AXES, None)
    return jax.shard_map(
        per_device,
        mesh=torus,
        in_specs=(rows, rows, rows, rows, rows, P(AXES)),
        out_specs=(rows, rows),
        check_vma=False,
    )
```

time: 934 us -> 85.7 us (0.09)
  waiting for transfers between devices: 439 us -> 0 us
  blocking collectives: 249 us -> 0 us
  local copies, waits for them, and re-layouts: 162 us -> 3.75 us
  Pallas kernels: 0 us -> 79.7 us
  matrix products: 39.3 us -> 0 us
  other arithmetic: 19.2 us -> 0 us
  between operations: 13.9 us -> 0.65 us
    reduce_scatter x1 -> x0, waiting for transfers between devices: 353 us -> none  [per_device(): lax.psum_scatter(lax.dot_general(tokens, grad_keys, (((0,), (0,)), ((), (...]
    all_gather x24 -> x0, blocking collectives: 249 us -> none  [stacked_from(): tiles = lax.all_gather(tiles, axes[k])]
    concatenate x5 -> x0, local copies, waits for them, and re-layouts: 112 us -> none  [the longest x4 111 us: gather_at_once(): return in_order(jnp.concatenate(outs, axis=widest + 1), dim)]
    all_gather x2 -> x0, waiting for transfers between devices: 86.2 us -> none  [the longest x1 86.2 us: per_device(): lax.all_gather(quarter, 'local', axis=0, tiled=True)]
    pallas_call x0 -> x1, Pallas kernels: none -> 79.7 us  [per_device(): pl.pallas_call(kernel, out_shape=(jax.ShapeDtypeStruct((TOK, D), BF), jax...]
    dot_general x6 -> x0, matrix products: 39.3 us -> none  [the longest x1 14.2 us: attend_back(): jnp.einsum('kgts,tkgd->skd', dscores, qmat, preferred_element_type=jnp.fl...]
    unnamed x15 -> x4, local copies, waits for them, and re-layouts: 22.1 us -> 3.75 us
    div x1 -> x0, other arithmetic: 12.9 us -> none  [attend_back(): probs = expo / jnp.sum(expo, axis=-1, keepdims=True)]
  transfers between devices with their start and end apart: 4 -> 0, of which waited for: 2 -> 0; matrix products, arithmetic and copies ran while one was open for 11% -> 0% of each run, Pallas kernels for 0% -> 0%
where the time goes in v1:
time: 85.7 us; the launch traced here: 84.1 us
  Pallas kernels  79.7 us (93%)
  local copies, waits for them, and re-layouts  3.75 us (4%)
    pallas_call x1, Pallas kernels, per_device(): pl.pallas_call(kernel, out_shape=(jax.ShapeDtypeStruct((TOK, D), BF), jax...  79.7 us
    unnamed x4, local copies, waits for them, and re-layouts  3.75 us

profile of v1, /device:TPU:2, one launch (start us, length us, event | category | flops | bytes accessed | tf_op | source)
XLA Modules:
  0.0 84.1 jit_solution(3133054329311659901)
XLA Ops:
  0.6 79.7 %key_backward.1 = (bf16[256,4096]{1,0:T(8,128)(2,1)}, f32[16,512]{1,0:T(8,128)}) custom-call(bf16[256,4096]{1,0:T(8,128)(2,1)} %tok_hbm.1, bf16[256,4096]{1,0:T(8,128)(2,1)} %q_hbm.1, bf16[256,512]{1,0:T(8,128)(2,1)} %v_hbm.1, bf16[256,4096]{1,0:T(8,128)(2,1)} %u_hbm.1, bf16[16,512]{1,0:T(8,128)(2,1)} %kw_hbm.1, s32[1,256]{1,0:T(1,128)} %bitcast.1), custom_call_target="tpu_custom_call" | custom-call | flops 5000000000 | bytes 9000000 | tf_op jit(solution)/shard_map/key_backward/pallas_call | solution.py:317
  80.3 0.0 copy-start
  80.3 3.1 %copy.10 = bf16[256,4096]{1,0:T(8,128)(2,1)} copy(bf16[256,4096]{1,0:T(8,128)(2,1)} %get-tuple-element.4) | data formatting | bytes 4194304
  83.5 0.0 copy-done
  83.5 0.6 copy.11
Async XLA Ops:
  80.3 3.1 %copy-start = (f32[16,512]{1,0:T(8,128)S(1)}, f32[16,512]{1,0:T(8,128)}, u32[]{:S(2)}) copy-start(f32[16,512]{1,0:T(8,128)} %get-tuple-element.5) | copy-start | bytes 98308

commit v2 on v1

--- a/solution.py
+++ b/solution.py
@@ -31,10 +31,10 @@
 
 def kernel(
     tok_hbm, q_hbm, v_hbm, u_hbm, kw_hbm, pos_hbm,
-    gt_hbm, gw_out,
-    tok, q, v, u, kw, pos, W, TT, cosine, sine, bias, keys, acc, gk, gt,
-    own, other, RC, A, RAE, RAO, B, RB, C, RZ,
-    load_sem, store_sem,
+    gt, gw_out,
+    SL, tok, q, v, u, kw, pos, W, TT, cosine, sine, bias, keys, acc, gk,
+    own, other, RC, A, RA, B, RB, C, RZ,
+    load_sem,
     zs, zr, s1s, s1r, s2s, s2r, cs, cr,
     rcs, rcr, ras, rar, rbs, rbr, rzs, rzr,
 ):
@@ -106,49 +106,54 @@
     for k in range(1, 8):
         wait(mine, zr.at[k - 1])
 
-    def first_slice(h):
-        return W.at[h, y, :, x, c]
-
-    def second_slice(h):
-        return W.at[h, y, :, :, c] if h % 2 == 0 else W.at[h, :, :, x, c]
+    def slopes(h):
+        def one(g, _):
+            n = h * GROUP + g
+            upper = u[:, pl.ds(pl.multiple_of(n * HEAD, HEAD), HEAD)]
+            full = dot_nt(v[:, h * HEAD : (h + 1) * HEAD], upper)
+            SL[n, :128] = full[:128, :128]
+            SL[n, 128:] = full[:, 128:]
+            return 0
+
+        lax.fori_loop(0, GROUP, one, 0, unroll=4)
+
+    def first_slice(s):
+        return W.at[:, y, s, x, c]
+
+    def second_slice(h, s):
+        return W.at[h, y, 0, :, c] if s == 0 else W.at[h, :, 1, x, c]
 
     def core_slice(h):
         return W.at[h, :, :, :, c]
 
+    for s in range(2):
+        for k in (1, 2, 3):
+            piece = first_slice(s)
+            send(piece, piece, s1s.at[s, k - 1], s1r.at[s, k - 1], (at_x, at_y)[s](k))
+    for copy in copies[3:]:
+        copy.wait()
+    slopes(0)
+    slopes(1)
+    for s in range(2):
+        for k in (1, 2, 3):
+            wait(first_slice(s), s1r.at[s, k - 1])
     for h in range(HEADS):
         for k in (1, 2, 3):
-            piece = first_slice(h)
-            send(piece, piece, s1s.at[h, k - 1], s1r.at[h, k - 1], at_x(k) if h % 2 == 0 else at_y(k))
-    for copy in copies[3:]:
-        copy.wait()
-    for h in range(HEADS):
-        for k in (1, 2, 3):
-            wait(first_slice(h), s1r.at[h, k - 1])
-        for k in (1, 2, 3):
-            piece = second_slice(h)
-            send(piece, piece, s2s.at[h, k - 1], s2r.at[h, k - 1], at_y(k) if h % 2 == 0 else at_x(k))
+            for s in range(2):
+                piece = second_slice(h, s)
+                send(piece, piece, s2s.at[h, s, k - 1], s2r.at[h, s, k - 1], (at_y, at_x)[s](k))
+    slopes(2)
+    slopes(3)
 
     def to_core(h):
-        for k in (1, 2, 3):
-            wait(second_slice(h), s2r.at[h, k - 1])
+        for s in range(2):
+            for k in (1, 2, 3):
+                wait(second_slice(h, s), s2r.at[h, s, k - 1])
         send(core_slice(h), core_slice(h), cs.at[h], cr.at[h], other_core)
 
     def r0(h):
         send(other.at[h], RC.at[h], rcs.at[h], rcr.at[h], other_core)
 
-    def a_slice(h, k):
-        if h % 2 == 0:
-            return A.at[h, lax.rem(y + k, 4)]
-        return A.at[h, :, :, lax.rem(x + k, 4)]
-
-    def b_slice(h, k):
-        if h % 2 == 0:
-            return B.at[h, :, lax.rem(x + k, 4)]
-        return B.at[h, :, lax.rem(y + k, 4)]
-
-    def ra_slot(h, k):
-        return (RAO if h % 2 else RAE).at[h // 2, k - 1]
-
     def r1(h):
         wait(RC.at[h], rcr.at[h])
 
@@ -158,34 +163,30 @@
 
         lax.fori_loop(0, 4, add, 0)
         for k in (1, 2, 3):
-            send(a_slice(h, k), ra_slot(h, k), ras.at[h, k - 1], rar.at[h, k - 1], at_y(k) if h % 2 == 0 else at_x(k))
+            for s in range(2):
+                piece = A.at[h, lax.rem(y + k, 4), 0] if s == 0 else A.at[h, :, 1, lax.rem(x + k, 4)]
+                send(piece, RA.at[h, s, k - 1], ras.at[h, s, k - 1], rar.at[h, s, k - 1], (at_y, at_x)[s](k))
 
     def r2(h):
-        for k in (1, 2, 3):
-            wait(ra_slot(h, k), rar.at[h, k - 1])
-        for i in range(2):
-            for j in range(4):
-                if h % 2 == 0:
-                    total = A[h, y, i, j].astype(F32)
-                    for k in range(3):
-                        total = total + RAE[h // 2, k, i, j].astype(F32)
-                else:
-                    total = A[h, j, i, x].astype(F32)
-                    for k in range(3):
-                        total = total + RAO[h // 2, k, j, i].astype(F32)
-                B[h, i, j] = total
-        for k in (1, 2, 3):
-            send(b_slice(h, k), RB.at[h, k - 1], rbs.at[h, k - 1], rbr.at[h, k - 1], at_x(k) if h % 2 == 0 else at_y(k))
+        for s in range(2):
+            for k in range(3):
+                wait(RA.at[h, s, k], rar.at[h, s, k])
+            total = (A[h, y, 0] if s == 0 else A[h, :, 1, x]).astype(F32)
+            for k in range(3):
+                total = total + RA[h, s, k].astype(F32)
+            B[h, s] = total
+            for k in (1, 2, 3):
+                piece = B.at[h, s, lax.rem((x, y)[s] + k, 4)]
+                send(piece, RB.at[h, s, k - 1], rbs.at[h, s, k - 1], rbr.at[h, s, k - 1], (at_x, at_y)[s](k))
 
     def r3(h):
-        for k in (1, 2, 3):
-            wait(RB.at[h, k - 1], rbr.at[h, k - 1])
-        me = x if h % 2 == 0 else y
-        for i in range(2):
-            total = B[h, i, me]
+        for s in range(2):
             for k in range(3):
-                total = total + RB[h, k, i]
-            C[h, i] = total.reshape(4, 16, HEAD)
+                wait(RB.at[h, s, k], rbr.at[h, s, k])
+            total = B[h, s, (x, y)[s]]
+            for k in range(3):
+                total = total + RB[h, s, k]
+            C[h, s] = total.reshape(4, 16, HEAD)
         for k in range(1, 8):
             there = lax.rem(z + k, 8)
             send(C.at[h, there // 4, lax.rem(there, 4)], RZ.at[h, k - 1], rzs.at[h, k - 1], rzr.at[h, k - 1], at_z(k))
@@ -211,17 +212,15 @@
         def one(g, _):
             lanes = pl.ds(pl.multiple_of((h * GROUP + g) * HEAD, HEAD), HEAD)
             queries = q[:, lanes]
-            upper = u[:, lanes]
             scores = dot_nt(keys[...], queries)
-            slopes = dot_nt(v[:, h * HEAD : (h + 1) * HEAD], upper)
             parts = []
             for b in range(2):
                 n = (b + 1) * 128
                 span = slice(b * 128, (b + 1) * 128)
                 s = scores[:n, span] + bias[:n, span]
                 top = jnp.max(s, axis=0, keepdims=True)
-                expo = jnp.exp((s - top) * SCALE)
-                sl = slopes[:n, span]
+                expo = jnp.exp2((s - top) * (SCALE * math.log2(math.e)))
+                sl = SL[h * GROUP + g, b * 128 : b * 128 + n]
                 norm = 1.0 / jnp.sum(expo, axis=0, keepdims=True)
                 inner = jnp.sum(expo * sl, axis=0, keepdims=True) * norm
                 parts.append((expo * (sl - inner) * (norm * SCALE)).astype(BF))
@@ -230,7 +229,7 @@
             acc[...] += dot(dscores, queries)
             return 0
 
-        lax.fori_loop(0, GROUP, one, 0)
+        lax.fori_loop(0, GROUP, one, 0, unroll=4)
 
     def weight(h):
         total = acc[...]
@@ -243,7 +242,7 @@
             other[h, i] = given.astype(BF).reshape(2, 4, 64, HEAD)
             return 0
 
-        lax.fori_loop(0, 4, give, 0)
+        lax.fori_loop(0, 4, give, 0, unroll=4)
         r0(h)
 
         def keep(i, _):
@@ -251,7 +250,7 @@
             own[h, i] = dot(TT[0, eight].reshape(512, TOK), mine).reshape(2, 4, 64, HEAD)
             return 0
 
-        lax.fori_loop(0, 4, keep, 0)
+        lax.fori_loop(0, 4, keep, 0, unroll=4)
 
     def tokens_part(i):
         def one(n, _):
@@ -261,8 +260,6 @@
             return 0
 
         lax.fori_loop(2 * i, 2 * i + 2, one, 0)
-        cols = pl.ds(i * 1024, 1024)
-        pltpu.make_async_copy(gt.at[:, cols], gt_hbm.at[:, cols], store_sem.at[i]).start()
 
     to_core(0)
     to_core(1)
@@ -293,62 +290,66 @@
     r4(2)
     r4(3)
 
+    for s in range(2):
+        for k in range(3):
+            wait(first_slice(s), s1s.at[s, k])
     for k in range(7):
         wait(mine, zs.at[k])
     for h in range(HEADS):
         for k in range(3):
-            wait(first_slice(h), s1s.at[h, k])
-            wait(second_slice(h), s2s.at[h, k])
-            wait(ra_slot(h, k + 1), ras.at[h, k])
-            wait(RB.at[h, k], rbs.at[h, k])
+            for s in range(2):
+                wait(second_slice(h, s), s2s.at[h, s, k])
+                wait(RA.at[h, s, k], ras.at[h, s, k])
+                wait(RB.at[h, s, k], rbs.at[h, s, k])
         wait(core_slice(h), cs.at[h])
         wait(RC.at[h], rcs.at[h])
         for k in range(7):
             wait(RZ.at[h, k], rzs.at[h, k])
-    for i in range(4):
-        cols = pl.ds(i * 1024, 1024)
-        wait(gt_hbm.at[:, cols], store_sem.at[i])
 
 
 def per_device(tokens, queries, values, upstream, key_weight, positions):
-    anywhere = pl.BlockSpec(memory_space=pl.ANY)
+    inputs = (tokens, queries, values, upstream, key_weight, positions.reshape(1, TOK))
+    far = pl.BlockSpec(memory_space=pltpu.HBM)
+    near = pl.BlockSpec(memory_space=pltpu.VMEM)
     dma = pltpu.SemaphoreType.DMA
     vm = pltpu.VMEM
     return pl.pallas_call(
         kernel,
-        out_shape=(jax.ShapeDtypeStruct((TOK, D), BF), jax.ShapeDtypeStruct((16, HEADS * HEAD), F32)),
-        in_specs=[anywhere] * 6,
-        out_specs=(anywhere, pl.BlockSpec(memory_space=pltpu.VMEM)),
+        out_shape=(pltpu.VMEM((TOK, D), BF), pltpu.VMEM((16, HEADS * HEAD), F32)),
+        in_specs=[far] * 6,
+        out_specs=(near, near),
         scratch_shapes=[
+            vm((HEADS * GROUP, 384, HEAD), F32),
             vm((TOK, D), BF), vm((TOK, D), BF), vm((TOK, HEADS * HEAD), BF), vm((TOK, D), BF),
             vm((16, HEADS * HEAD), BF), vm((1, TOK), jnp.int32),
             vm((HEADS, 4, 2, 4, 2, 4, 16, HEAD), BF),
             vm((2, 32, 64, TOK), BF),
             vm((TOK, HEAD), F32), vm((TOK, HEAD), F32), vm((TOK, TOK), F32),
-            vm((TOK, HEAD), BF), vm((TOK, HEAD), F32), vm((TOK, HEADS * HEAD), BF), vm((TOK, D), BF),
+            vm((TOK, HEAD), BF), vm((TOK, HEAD), F32), vm((TOK, HEADS * HEAD), BF),
             vm((HEADS, 4, 2, 4, 64, HEAD), F32),
             vm((HEADS, 4, 2, 4, 64, HEAD), BF),
             vm((HEADS, 4, 2, 4, 64, HEAD), BF),
             vm((HEADS, 4, 2, 4, 64, HEAD), BF),
-            vm((2, 3, 2, 4, 64, HEAD), BF), vm((2, 3, 4, 2, 64, HEAD), BF),
+            vm((HEADS, 2, 3, 4, 64, HEAD), BF),
             vm((HEADS, 2, 4, 64, HEAD), F32),
-            vm((HEADS, 3, 2, 64, HEAD), F32),
+            vm((HEADS, 2, 3, 64, HEAD), F32),
             vm((HEADS, 2, 4, 16, HEAD), F32),
             vm((HEADS, 7, 16, HEAD), F32),
-            dma((6,)), dma((4,)),
-            dma((7,)), dma((7,)), dma((HEADS, 3)), dma((HEADS, 3)), dma((HEADS, 3)), dma((HEADS, 3)),
+            dma((6,)),
+            dma((7,)), dma((7,)), dma((2, 3)), dma((2, 3)), dma((HEADS, 2, 3)), dma((HEADS, 2, 3)),
             dma((HEADS,)), dma((HEADS,)),
-            dma((HEADS,)), dma((HEADS,)), dma((HEADS, 3)), dma((HEADS, 3)), dma((HEADS, 3)), dma((HEADS, 3)),
+            dma((HEADS,)), dma((HEADS,)),
+            dma((HEADS, 2, 3)), dma((HEADS, 2, 3)), dma((HEADS, 2, 3)), dma((HEADS, 2, 3)),
             dma((HEADS, 7)), dma((HEADS, 7)),
         ],
         compiler_params=pltpu.CompilerParams(
-            collective_id=0, has_side_effects=True, vmem_limit_bytes=56 << 20
+            collective_id=0, has_side_effects=True, vmem_limit_bytes=48 << 20
         ),
         cost_estimate=pl.CostEstimate(
             flops=5_000_000_000, bytes_accessed=9_000_000, transcendentals=2_000_000
         ),
         name="key_backward",
-    )(tokens, queries, values, upstream, key_weight, positions.reshape(1, TOK))
+    )(*(pltpu.with_memory_space_constraint(a, pltpu.HBM) for a in inputs))
 
 
 def solution(mesh):

time: 85.7 us -> 67.7 us (0.79); the launches traced: 84.1 us -> 67.5 us
  Pallas kernels: 79.7 us -> 64.9 us
  local copies, waits for them, and re-layouts: 3.75 us -> 1.94 us
    pallas_call x1, Pallas kernels: 79.7 us -> 64.9 us  [per_device(): pl.pallas_call(kernel, out_shape=(pltpu.VMEM((TOK, D), BF), pltpu.VMEM((1...]
    unnamed x4 -> x2, local copies, waits for them, and re-layouts: 3.75 us -> 1.94 us
where the time goes in v2:
time: 67.7 us; the launch traced here: 67.5 us
  Pallas kernels  64.9 us (96%)
  local copies, waits for them, and re-layouts  1.94 us (3%)
    pallas_call x1, Pallas kernels, per_device(): pl.pallas_call(kernel, out_shape=(pltpu.VMEM((TOK, D), BF), pltpu.VMEM((1...  64.9 us
    unnamed x2, local copies, waits for them, and re-layouts  1.94 us

profile of v2, /device:TPU:2, one launch (start us, length us, event | category | flops | bytes accessed | tf_op | source)
XLA Modules:
  0.0 67.5 jit_solution(1902278145613989888)
XLA Ops:
  0.6 64.9 %key_backward.1 = (bf16[256,4096]{1,0:T(8,128)(2,1)S(1)}, f32[16,512]{1,0:T(8,128)S(1)}) custom-call(bf16[256,4096]{1,0:T(8,128)(2,1)} %tok_hbm.1, bf16[256,4096]{1,0:T(8,128)(2,1)} %q_hbm.1, bf16[256,512]{1,0:T(8,128)(2,1)} %v_hbm.1, bf16[256,4096]{1,0:T(8,128)(2,1)} %u_hbm.1, bf16[16,512]{1,0:T(8,128)(2,1)} %kw_hbm.1, s32[1,256]{1,0:T(1,128)} %bitcast.1), custom_call_target="tpu_custom_call" | custom-call | flops 5000000000 | bytes 9000000 | tf_op jit(solution)/shard_map/key_backward/pallas_call | solution.py:316
  65.6 1.3 %copy.10 = bf16[256,4096]{1,0:T(8,128)(2,1)} copy(bf16[256,4096]{1,0:T(8,128)(2,1)S(1)} %get-tuple-element.2) | data formatting | bytes 4194304
  66.9 0.6 copy.11

commit v3 on v2

--- a/solution.py
+++ b/solution.py
@@ -75,9 +75,11 @@
         W[h, y, zh, x, c, zl] = kw[:, h * HEAD : (h + 1) * HEAD]
     pl.semaphore_wait(barrier, len(peers))
 
-    mine = W.at[:, y, zh, x, c, zl]
-    for k in range(1, 8):
-        send(mine, mine, zs.at[k - 1], zr.at[k - 1], at_z(k))
+    spans = (slice(0, 1), slice(1, HEADS))
+    mine = [W.at[span, y, zh, x, c, zl] for span in spans]
+    for p in range(2):
+        for k in range(1, 8):
+            send(mine[p], mine[p], zs.at[p, k - 1], zr.at[p, k - 1], at_z(k))
 
     copies[1].wait()
     lane = lax.broadcasted_iota(jnp.int32, (1, HEAD), 1)
@@ -103,9 +105,6 @@
 
     lax.fori_loop(0, 32, turn, 0)
 
-    for k in range(1, 8):
-        wait(mine, zr.at[k - 1])
-
     def slopes(h):
         def one(g, _):
             n = h * GROUP + g
@@ -117,8 +116,8 @@
 
         lax.fori_loop(0, GROUP, one, 0, unroll=4)
 
-    def first_slice(s):
-        return W.at[:, y, s, x, c]
+    def first_slice(p, s):
+        return W.at[spans[p], y, s, x, c]
 
     def second_slice(h, s):
         return W.at[h, y, 0, :, c] if s == 0 else W.at[h, :, 1, x, c]
@@ -126,29 +125,44 @@
     def core_slice(h):
         return W.at[h, :, :, :, c]
 
-    for s in range(2):
+    three = pl.ds(0, 3)
+
+    def first_slots(p, s):
+        return W.at[spans[p], y, s, three, c]
+
+    def second_slots(h, s):
+        return W.at[h, three, 0, :, c] if s == 0 else W.at[h, :, 1, three, c]
+
+    def first_stage(p):
+        for k in range(7):
+            wait(mine[p], zr.at[p, k])
         for k in (1, 2, 3):
-            piece = first_slice(s)
-            send(piece, piece, s1s.at[s, k - 1], s1r.at[s, k - 1], (at_x, at_y)[s](k))
+            for s in range(2):
+                piece = first_slice(p, s)
+                send(piece, piece, s1s.at[p, s], s1r.at[p, s], (at_x, at_y)[s](k))
+
+    def second_stage(p):
+        for s in range(2):
+            wait(first_slots(p, s), s1r.at[p, s])
+        for h in range(HEADS)[spans[p]]:
+            for k in (1, 2, 3):
+                for s in range(2):
+                    piece = second_slice(h, s)
+                    send(piece, piece, s2s.at[h, s], s2r.at[h, s], (at_y, at_x)[s](k))
+
+    first_stage(0)
+    first_stage(1)
     for copy in copies[3:]:
         copy.wait()
     slopes(0)
+    second_stage(0)
+    second_stage(1)
     slopes(1)
-    for s in range(2):
-        for k in (1, 2, 3):
-            wait(first_slice(s), s1r.at[s, k - 1])
-    for h in range(HEADS):
-        for k in (1, 2, 3):
-            for s in range(2):
-                piece = second_slice(h, s)
-                send(piece, piece, s2s.at[h, s, k - 1], s2r.at[h, s, k - 1], (at_y, at_x)[s](k))
     slopes(2)
-    slopes(3)
 
     def to_core(h):
         for s in range(2):
-            for k in (1, 2, 3):
-                wait(second_slice(h, s), s2r.at[h, s, k - 1])
+            wait(second_slots(h, s), s2r.at[h, s])
         send(core_slice(h), core_slice(h), cs.at[h], cr.at[h], other_core)
 
     def r0(h):
@@ -165,39 +179,44 @@
         for k in (1, 2, 3):
             for s in range(2):
                 piece = A.at[h, lax.rem(y + k, 4), 0] if s == 0 else A.at[h, :, 1, lax.rem(x + k, 4)]
-                send(piece, RA.at[h, s, k - 1], ras.at[h, s, k - 1], rar.at[h, s, k - 1], (at_y, at_x)[s](k))
+                send(piece, RA.at[h, s, k - 1], ras.at[h, s], rar.at[h, s], (at_y, at_x)[s](k))
 
     def r2(h):
         for s in range(2):
-            for k in range(3):
-                wait(RA.at[h, s, k], rar.at[h, s, k])
+            wait(RA.at[h, s], rar.at[h, s])
             total = (A[h, y, 0] if s == 0 else A[h, :, 1, x]).astype(F32)
             for k in range(3):
                 total = total + RA[h, s, k].astype(F32)
             B[h, s] = total
-            for k in (1, 2, 3):
-                piece = B.at[h, s, lax.rem((x, y)[s] + k, 4)]
-                send(piece, RB.at[h, s, k - 1], rbs.at[h, s, k - 1], rbr.at[h, s, k - 1], (at_x, at_y)[s](k))
-
-    def r3(h):
-        for s in range(2):
-            for k in range(3):
-                wait(RB.at[h, s, k], rbr.at[h, s, k])
-            total = B[h, s, (x, y)[s]]
-            for k in range(3):
-                total = total + RB[h, s, k]
-            C[h, s] = total.reshape(4, 16, HEAD)
+
+    sets = (slice(0, 2), slice(2, 3), slice(3, 4))
+
+    def to_second(n):
+        for k in (1, 2, 3):
+            for s in range(2):
+                piece = B.at[sets[n], s, lax.rem((x, y)[s] + k, 4)]
+                send(piece, RB.at[sets[n], s, k - 1], rbs.at[n, s], rbr.at[n, s], (at_x, at_y)[s](k))
+
+    def r3(n):
+        for s in range(2):
+            wait(RB.at[sets[n], s], rbr.at[n, s])
+            for h in range(HEADS)[sets[n]]:
+                total = B[h, s, (x, y)[s]]
+                for k in range(3):
+                    total = total + RB[h, s, k]
+                C[h, s] = total.reshape(4, 16, HEAD)
         for k in range(1, 8):
             there = lax.rem(z + k, 8)
-            send(C.at[h, there // 4, lax.rem(there, 4)], RZ.at[h, k - 1], rzs.at[h, k - 1], rzr.at[h, k - 1], at_z(k))
-
-    def r4(h):
-        for k in range(1, 8):
-            wait(RZ.at[h, k - 1], rzr.at[h, k - 1])
-        total = C[h, zh, zl]
-        for k in range(7):
-            total = total + RZ[h, k]
-        gw_out[:, h * HEAD : (h + 1) * HEAD] = total
+            piece = C.at[sets[n], there // 4, lax.rem(there, 4)]
+            send(piece, RZ.at[sets[n], k - 1], rzs.at[n], rzr.at[n], at_z(k))
+
+    def r4(n):
+        wait(RZ.at[sets[n]], rzr.at[n])
+        for h in range(HEADS)[sets[n]]:
+            total = C[h, zh, zl]
+            for k in range(7):
+                total = total + RZ[h, k]
+            gw_out[:, h * HEAD : (h + 1) * HEAD] = total
 
     def project(h):
         wait(core_slice(h), cr.at[h])
@@ -229,7 +248,7 @@
             acc[...] += dot(dscores, queries)
             return 0
 
-        lax.fori_loop(0, GROUP, one, 0, unroll=4)
+        lax.fori_loop(0, GROUP, one, 0, unroll=8)
 
     def weight(h):
         total = acc[...]
@@ -252,59 +271,69 @@
 
         lax.fori_loop(0, 4, keep, 0, unroll=4)
 
-    def tokens_part(i):
+    def tokens_part(i, j):
         def one(n, _):
             rows = [W[h, n // 2, n % 2].reshape(512, HEAD) for h in range(HEADS)]
             cols = pl.ds(pl.multiple_of(n * 512, 512), 512)
             gt[:, cols] = dot_nt(gk[...], jnp.concatenate(rows, axis=1)).astype(BF)
             return 0
 
-        lax.fori_loop(2 * i, 2 * i + 2, one, 0)
+        lax.fori_loop(i, j, one, 0)
 
     to_core(0)
-    to_core(1)
+    slopes(3)
     for h in range(HEADS):
         project(h)
-        if h + 2 < HEADS:
-            to_core(h + 2)
+        if h == 0:
+            to_core(1)
+            to_core(2)
+        elif h == 1:
+            to_core(3)
         attend(h)
         if h >= 1:
             r1(h - 1)
+        if h >= 3:
+            r2(h - 3)
         weight(h)
-        if h >= 2:
-            r2(h - 2)
-        if h >= 3:
-            r3(h - 3)
-    tokens_part(0)
+
+    def gather_sent():
+        for p in range(2):
+            for k in range(7):
+                wait(mine[p], zs.at[p, k])
+            for s in range(2):
+                wait(first_slots(p, s), s1s.at[p, s])
+        for h in range(HEADS):
+            for s in range(2):
+                wait(second_slots(h, s), s2s.at[h, s])
+            wait(core_slice(h), cs.at[h])
+
+    r2(1)
+    to_second(0)
+    tokens_part(0, 2)
     r1(3)
+    tokens_part(2, 5)
     r2(2)
+    to_second(1)
+    r3(0)
+    tokens_part(5, 7)
+    r2(3)
+    to_second(2)
+    tokens_part(7, 8)
+    gather_sent()
     r3(1)
-    tokens_part(1)
-    tokens_part(2)
-    r2(3)
     r3(2)
+    for h in range(HEADS):
+        wait(RC.at[h], rcs.at[h])
+        for s in range(2):
+            wait(RA.at[h, s], ras.at[h, s])
+    for n in range(3):
+        for s in range(2):
+            wait(RB.at[sets[n], s], rbs.at[n, s])
     r4(0)
     r4(1)
-    tokens_part(3)
-    r3(3)
     r4(2)
-    r4(3)
-
-    for s in range(2):
-        for k in range(3):
-            wait(first_slice(s), s1s.at[s, k])
-    for k in range(7):
-        wait(mine, zs.at[k])
-    for h in range(HEADS):
-        for k in range(3):
-            for s in range(2):
-                wait(second_slice(h, s), s2s.at[h, s, k])
-                wait(RA.at[h, s, k], ras.at[h, s, k])
-                wait(RB.at[h, s, k], rbs.at[h, s, k])
-        wait(core_slice(h), cs.at[h])
-        wait(RC.at[h], rcs.at[h])
-        for k in range(7):
-            wait(RZ.at[h, k], rzs.at[h, k])
+    for n in range(3):
+        wait(RZ.at[sets[n]], rzs.at[n])
 
 
 def per_device(tokens, queries, values, upstream, key_weight, positions):
@@ -336,11 +365,11 @@
             vm((HEADS, 2, 4, 16, HEAD), F32),
             vm((HEADS, 7, 16, HEAD), F32),
             dma((6,)),
-            dma((7,)), dma((7,)), dma((2, 3)), dma((2, 3)), dma((HEADS, 2, 3)), dma((HEADS, 2, 3)),
+            dma((2, 7)), dma((2, 7)), dma((2, 2)), dma((2, 2)), dma((HEADS, 2)), dma((HEADS, 2)),
             dma((HEADS,)), dma((HEADS,)),
             dma((HEADS,)), dma((HEADS,)),
-            dma((HEADS, 2, 3)), dma((HEADS, 2, 3)), dma((HEADS, 2, 3)), dma((HEADS, 2, 3)),
-            dma((HEADS, 7)), dma((HEADS, 7)),
+            dma((HEADS, 2)), dma((HEADS, 2)), dma((3, 2)), dma((3, 2)),
+            dma((3,)), dma((3,)),
         ],
         compiler_params=pltpu.CompilerParams(
             collective_id=0, has_side_effects=True, vmem_limit_bytes=48 << 20

time: 67.7 us -> 63.7 us (0.941)
  Pallas kernels: 64.9 us -> 60.9 us
    pallas_call x1, Pallas kernels: 64.9 us -> 60.9 us  [per_device(): pl.pallas_call(kernel, out_shape=(pltpu.VMEM((TOK, D), BF), pltpu.VMEM((1...]
where the time goes in v3:
time: 63.7 us; the launch traced here: 63.5 us
  Pallas kernels  60.9 us (96%)
  local copies, waits for them, and re-layouts  1.94 us (3%)
  between operations  0.64 us (1%)
    pallas_call x1, Pallas kernels, per_device(): pl.pallas_call(kernel, out_shape=(pltpu.VMEM((TOK, D), BF), pltpu.VMEM((1...  60.9 us
    unnamed x2, local copies, waits for them, and re-layouts  1.94 us

profile of v3, /device:TPU:2, one launch (start us, length us, event | category | flops | bytes accessed | tf_op | source)
XLA Modules:
  0.0 63.5 jit_solution(8409732016950404388)
XLA Ops:
  0.6 60.9 %key_backward.1 = (bf16[256,4096]{1,0:T(8,128)(2,1)S(1)}, f32[16,512]{1,0:T(8,128)S(1)}) custom-call(bf16[256,4096]{1,0:T(8,128)(2,1)} %tok_hbm.1, bf16[256,4096]{1,0:T(8,128)(2,1)} %q_hbm.1, bf16[256,512]{1,0:T(8,128)(2,1)} %v_hbm.1, bf16[256,4096]{1,0:T(8,128)(2,1)} %u_hbm.1, bf16[16,512]{1,0:T(8,128)(2,1)} %kw_hbm.1, s32[1,256]{1,0:T(1,128)} %bitcast.1), custom_call_target="tpu_custom_call" | custom-call | flops 5000000000 | bytes 9000000 | tf_op jit(solution)/shard_map/key_backward/pallas_call | solution.py:345
  61.6 1.3 %copy.10 = bf16[256,4096]{1,0:T(8,128)(2,1)} copy(bf16[256,4096]{1,0:T(8,128)(2,1)S(1)} %get-tuple-element.2) | data formatting | bytes 4194304
  62.9 0.6 copy.11

commit v4 on v3

--- a/solution.py
+++ b/solution.py
@@ -18,6 +18,8 @@
 SCALE = HEAD**-0.5
 BF = jnp.bfloat16
 F32 = jnp.float32
+FAR4 = (2, 1, 3)
+FAR8 = (4, 3, 5, 2, 6, 1, 7)
 NT = (((1,), (1,)), ((), ()))
 
 
@@ -61,15 +63,14 @@
     def wait(like, sem):
         pltpu.make_async_copy(like, like, sem).wait()
 
+    barrier = pltpu.get_barrier_semaphore()
+    peers = [at_z(k) for k in FAR8] + [f(k) for k in FAR4 for f in (at_x, at_y)] + [other_core]
+    for peer in peers:
+        pl.semaphore_signal(barrier, inc=1, device_id=peer, device_id_type=MESH)
     loads = [(kw_hbm, kw), (pos_hbm, pos), (tok_hbm, tok), (v_hbm, v), (q_hbm, q), (u_hbm, u)]
     copies = [pltpu.make_async_copy(a, b, load_sem.at[i]) for i, (a, b) in enumerate(loads)]
     for copy in copies:
         copy.start()
-    barrier = pltpu.get_barrier_semaphore()
-    peers = [other_core] + [at_x(k) for k in (1, 2, 3)] + [at_y(k) for k in (1, 2, 3)]
-    peers += [at_z(k) for k in range(1, 8)]
-    for peer in peers:
-        pl.semaphore_signal(barrier, inc=1, device_id=peer, device_id_type=MESH)
     copies[0].wait()
     for h in range(HEADS):
         W[h, y, zh, x, c, zl] = kw[:, h * HEAD : (h + 1) * HEAD]
@@ -78,7 +79,7 @@
     spans = (slice(0, 1), slice(1, HEADS))
     mine = [W.at[span, y, zh, x, c, zl] for span in spans]
     for p in range(2):
-        for k in range(1, 8):
+        for k in FAR8:
             send(mine[p], mine[p], zs.at[p, k - 1], zr.at[p, k - 1], at_z(k))
 
     copies[1].wait()
@@ -136,7 +137,7 @@
     def first_stage(p):
         for k in range(7):
             wait(mine[p], zr.at[p, k])
-        for k in (1, 2, 3):
+        for k in FAR4:
             for s in range(2):
                 piece = first_slice(p, s)
                 send(piece, piece, s1s.at[p, s], s1r.at[p, s], (at_x, at_y)[s](k))
@@ -145,7 +146,7 @@
         for s in range(2):
             wait(first_slots(p, s), s1r.at[p, s])
         for h in range(HEADS)[spans[p]]:
-            for k in (1, 2, 3):
+            for k in FAR4:
                 for s in range(2):
                     piece = second_slice(h, s)
                     send(piece, piece, s2s.at[h, s], s2r.at[h, s], (at_y, at_x)[s](k))
@@ -176,7 +177,7 @@
             return 0
 
         lax.fori_loop(0, 4, add, 0)
-        for k in (1, 2, 3):
+        for k in FAR4:
             for s in range(2):
                 piece = A.at[h, lax.rem(y + k, 4), 0] if s == 0 else A.at[h, :, 1, lax.rem(x + k, 4)]
                 send(piece, RA.at[h, s, k - 1], ras.at[h, s], rar.at[h, s], (at_y, at_x)[s](k))
@@ -192,7 +193,7 @@
     sets = (slice(0, 2), slice(2, 3), slice(3, 4))
 
     def to_second(n):
-        for k in (1, 2, 3):
+        for k in FAR4:
             for s in range(2):
                 piece = B.at[sets[n], s, lax.rem((x, y)[s] + k, 4)]
                 send(piece, RB.at[sets[n], s, k - 1], rbs.at[n, s], rbr.at[n, s], (at_x, at_y)[s](k))
@@ -205,7 +206,7 @@
                 for k in range(3):
                     total = total + RB[h, s, k]
                 C[h, s] = total.reshape(4, 16, HEAD)
-        for k in range(1, 8):
+        for k in FAR8:
             there = lax.rem(z + k, 8)
             piece = C.at[sets[n], there // 4, lax.rem(there, 4)]
             send(piece, RZ.at[sets[n], k - 1], rzs.at[n], rzr.at[n], at_z(k))
@@ -218,12 +219,16 @@
                 total = total + RZ[h, k]
             gw_out[:, h * HEAD : (h + 1) * HEAD] = total
 
-    def project(h):
-        wait(core_slice(h), cr.at[h])
-        total = jnp.zeros((TOK, HEAD), F32)
+    def project(*heads):
+        for h in heads:
+            wait(core_slice(h), cr.at[h])
+        total = jnp.zeros((TOK, len(heads) * HEAD), F32)
         for i in range(4):
-            total = total + dot(tok[:, i * 1024 : (i + 1) * 1024], W[h, i].reshape(1024, HEAD))
-        keys[...] = (total * cosine[...] + pltpu.roll(total, half, 1) * sine[...]).astype(BF)
+            rows = jnp.concatenate([W[h, i].reshape(1024, HEAD) for h in heads], axis=1)
+            total = total + dot(tok[:, i * 1024 : (i + 1) * 1024], rows)
+        for i, h in enumerate(heads):
+            raw = total[:, i * HEAD : (i + 1) * HEAD]
+            keys[h] = (raw * cosine[...] + pltpu.roll(raw, half, 1) * sine[...]).astype(BF)
 
     def attend(h):
         acc[...] = jnp.zeros_like(acc)
@@ -231,7 +236,7 @@
         def one(g, _):
             lanes = pl.ds(pl.multiple_of((h * GROUP + g) * HEAD, HEAD), HEAD)
             queries = q[:, lanes]
-            scores = dot_nt(keys[...], queries)
+            scores = dot_nt(keys[h], queries)
             parts = []
             for b in range(2):
                 n = (b + 1) * 128
@@ -283,7 +288,10 @@
     to_core(0)
     slopes(3)
     for h in range(HEADS):
-        project(h)
+        if h < 2:
+            project(h)
+        elif h == 2:
+            project(2, 3)
         if h == 0:
             to_core(1)
             to_core(2)
@@ -336,13 +344,21 @@
         wait(RZ.at[sets[n]], rzs.at[n])
 
 
+def hand_over(gt, gw, gt_hbm, gw_hbm, sem):
+    copies = [pltpu.make_async_copy(a, b, sem.at[i]) for i, (a, b) in enumerate(((gw, gw_hbm), (gt, gt_hbm)))]
+    for copy in copies:
+        copy.start()
+    for copy in copies:
+        copy.wait()
+
+
 def per_device(tokens, queries, values, upstream, key_weight, positions):
     inputs = (tokens, queries, values, upstream, key_weight, positions.reshape(1, TOK))
     far = pl.BlockSpec(memory_space=pltpu.HBM)
     near = pl.BlockSpec(memory_space=pltpu.VMEM)
     dma = pltpu.SemaphoreType.DMA
     vm = pltpu.VMEM
-    return pl.pallas_call(
+    results = pl.pallas_call(
         kernel,
         out_shape=(pltpu.VMEM((TOK, D), BF), pltpu.VMEM((16, HEADS * HEAD), F32)),
         in_specs=[far] * 6,
@@ -354,7 +370,7 @@
             vm((HEADS, 4, 2, 4, 2, 4, 16, HEAD), BF),
             vm((2, 32, 64, TOK), BF),
             vm((TOK, HEAD), F32), vm((TOK, HEAD), F32), vm((TOK, TOK), F32),
-            vm((TOK, HEAD), BF), vm((TOK, HEAD), F32), vm((TOK, HEADS * HEAD), BF),
+            vm((HEADS, TOK, HEAD), BF), vm((TOK, HEAD), F32), vm((TOK, HEADS * HEAD), BF),
             vm((HEADS, 4, 2, 4, 64, HEAD), F32),
             vm((HEADS, 4, 2, 4, 64, HEAD), BF),
             vm((HEADS, 4, 2, 4, 64, HEAD), BF),
@@ -379,6 +395,14 @@
         ),
         name="key_backward",
     )(*(pltpu.with_memory_space_constraint(a, pltpu.HBM) for a in inputs))
+    return pl.pallas_call(
+        hand_over,
+        out_shape=(jax.ShapeDtypeStruct((TOK, D), BF), jax.ShapeDtypeStruct((16, HEADS * HEAD), F32)),
+        in_specs=[near] * 2,
+        out_specs=(far, far),
+        scratch_shapes=[dma((2,))],
+        name="hand_over",
+    )(*(pltpu.with_memory_space_constraint(a, pltpu.VMEM) for a in results))
 
 
 def solution(mesh):

time: 63.7 us -> 62.7 us (0.984)
  local copies, waits for them, and re-layouts: 1.94 us -> 0 us
  Pallas kernels: 60.9 us -> 61.9 us
    unnamed x2 -> x0, local copies, waits for them, and re-layouts: 1.94 us -> none
    pallas_call x0 -> x1, Pallas kernels: none -> 1.35 us  [per_device(): pl.pallas_call(hand_over, out_shape=(jax.ShapeDtypeStruct((TOK, D), BF),...]
where the time goes in v4:
time: 62.7 us; the launch traced here: 62.6 us
  Pallas kernels  61.9 us (99%)
  between operations  0.64 us (1%)
    pallas_call x1, Pallas kernels, per_device(): pl.pallas_call(kernel, out_shape=(pltpu.VMEM((TOK, D), BF), pltpu.VMEM((1...  60.6 us
    pallas_call x1, Pallas kernels, per_device(): pl.pallas_call(hand_over, out_shape=(jax.ShapeDtypeStruct((TOK, D), BF),...  1.35 us

profile of v4, /device:TPU:2, one launch (start us, length us, event | category | flops | bytes accessed | tf_op | source)
XLA Modules:
  0.0 62.6 jit_solution(10906088954411173366)
XLA Ops:
  0.6 60.6 %key_backward.1 = (bf16[256,4096]{1,0:T(8,128)(2,1)S(1)}, f32[16,512]{1,0:T(8,128)S(1)}) custom-call(bf16[256,4096]{1,0:T(8,128)(2,1)} %tok_hbm.1, bf16[256,4096]{1,0:T(8,128)(2,1)} %q_hbm.1, bf16[256,512]{1,0:T(8,128)(2,1)} %v_hbm.1, bf16[256,4096]{1,0:T(8,128)(2,1)} %u_hbm.1, bf16[16,512]{1,0:T(8,128)(2,1)} %kw_hbm.1, s32[1,256]{1,0:T(1,128)} %bitcast.1), custom_call_target="tpu_custom_call" | custom-call | flops 5000000000 | bytes 9000000 | tf_op jit(solution)/shard_map/key_backward/pallas_call | solution.py:361
  61.2 1.3 %hand_over.1 = (bf16[256,4096]{1,0:T(8,128)(2,1)}, f32[16,512]{1,0:T(8,128)}) custom-call(bf16[256,4096]{1,0:T(8,128)(2,1)S(1)} %get-tuple-element.4.gt, f32[16,512]{1,0:T(8,128)S(1)} %get-tuple-element.5.gw), custom_call_target="tpu_custom_call" | custom-call | tf_op jit(solution)/shard_map/hand_over/pallas_call | solution.py:398

commit v5 on v4

--- a/solution.py
+++ b/solution.py
@@ -288,10 +288,7 @@
     to_core(0)
     slopes(3)
     for h in range(HEADS):
-        if h < 2:
-            project(h)
-        elif h == 2:
-            project(2, 3)
+        project(h)
         if h == 0:
             to_core(1)
             to_core(2)
@@ -300,8 +297,6 @@
         attend(h)
         if h >= 1:
             r1(h - 1)
-        if h >= 3:
-            r2(h - 3)
         weight(h)
 
     def gather_sent():
@@ -315,11 +310,12 @@
                 wait(second_slots(h, s), s2s.at[h, s])
             wait(core_slice(h), cs.at[h])
 
+    r2(0)
     r2(1)
     to_second(0)
-    tokens_part(0, 2)
+    tokens_part(0, 1)
     r1(3)
-    tokens_part(2, 5)
+    tokens_part(1, 5)
     r2(2)
     to_second(1)
     r3(0)
@@ -345,7 +341,10 @@
 
 
 def hand_over(gt, gw, gt_hbm, gw_hbm, sem):
-    copies = [pltpu.make_async_copy(a, b, sem.at[i]) for i, (a, b) in enumerate(((gw, gw_hbm), (gt, gt_hbm)))]
+    copies = [pltpu.make_async_copy(gw, gw_hbm, sem.at[4])]
+    for i in range(4):
+        rows = pl.ds(i * 64, 64)
+        copies.append(pltpu.make_async_copy(gt.at[rows], gt_hbm.at[rows], sem.at[i]))
     for copy in copies:
         copy.start()
     for copy in copies:
@@ -400,7 +399,7 @@
         out_shape=(jax.ShapeDtypeStruct((TOK, D), BF), jax.ShapeDtypeStruct((16, HEADS * HEAD), F32)),
         in_specs=[near] * 2,
         out_specs=(far, far),
-        scratch_shapes=[dma((2,))],
+        scratch_shapes=[dma((5,))],
         name="hand_over",
     )(*(pltpu.with_memory_space_constraint(a, pltpu.VMEM) for a in results))
 

time: 62.7 us -> 61 us (0.973)
  Pallas kernels: 61.9 us -> 60.2 us
    pallas_call x1, Pallas kernels: 60.6 us -> 58.9 us  [per_device(): pl.pallas_call(kernel, out_shape=(pltpu.VMEM((TOK, D), BF), pltpu.VMEM((1...]
where the time goes in v5:
time: 61 us; the launch traced here: 60.9 us
  Pallas kernels  60.2 us (99%)
  between operations  0.64 us (1%)
    pallas_call x1, Pallas kernels, per_device(): pl.pallas_call(kernel, out_shape=(pltpu.VMEM((TOK, D), BF), pltpu.VMEM((1...  58.9 us
    pallas_call x1, Pallas kernels, per_device(): pl.pallas_call(hand_over, out_shape=(jax.ShapeDtypeStruct((TOK, D), BF),...  1.37 us

profile of v5, /device:TPU:2, one launch (start us, length us, event | category | flops | bytes accessed | tf_op | source)
XLA Modules:
  0.0 60.9 jit_solution(4589674540476411240)
XLA Ops:
  0.6 58.9 %key_backward.1 = (bf16[256,4096]{1,0:T(8,128)(2,1)S(1)}, f32[16,512]{1,0:T(8,128)S(1)}) custom-call(bf16[256,4096]{1,0:T(8,128)(2,1)} %tok_hbm.1, bf16[256,4096]{1,0:T(8,128)(2,1)} %q_hbm.1, bf16[256,512]{1,0:T(8,128)(2,1)} %v_hbm.1, bf16[256,4096]{1,0:T(8,128)(2,1)} %u_hbm.1, bf16[16,512]{1,0:T(8,128)(2,1)} %kw_hbm.1, s32[1,256]{1,0:T(1,128)} %bitcast.1), custom_call_target="tpu_custom_call" | custom-call | flops 5000000000 | bytes 9000000 | tf_op jit(solution)/shard_map/key_backward/pallas_call | solution.py:360
  59.5 1.4 %hand_over.1 = (bf16[256,4096]{1,0:T(8,128)(2,1)}, f32[16,512]{1,0:T(8,128)}) custom-call(bf16[256,4096]{1,0:T(8,128)(2,1)S(1)} %get-tuple-element.4.gt, f32[16,512]{1,0:T(8,128)S(1)} %get-tuple-element.5.gw), custom_call_target="tpu_custom_call" | custom-call | tf_op jit(solution)/shard_map/hand_over/pallas_call | solution.py:397

commit v6 on v5

--- a/solution.py
+++ b/solution.py
@@ -313,9 +313,8 @@
     r2(0)
     r2(1)
     to_second(0)
-    tokens_part(0, 1)
     r1(3)
-    tokens_part(1, 5)
+    tokens_part(0, 5)
     r2(2)
     to_second(1)
     r3(0)

time: 61 us -> 61 us (level)
  no operation moved by 1% of the time
where the time goes in v6:
time: 61 us; the launch traced here: 60.9 us
  Pallas kernels  60.2 us (99%)
  between operations  0.64 us (1%)
    pallas_call x1, Pallas kernels, per_device(): pl.pallas_call(kernel, out_shape=(pltpu.VMEM((TOK, D), BF), pltpu.VMEM((1...  58.9 us
    pallas_call x1, Pallas kernels, per_device(): pl.pallas_call(hand_over, out_shape=(jax.ShapeDtypeStruct((TOK, D), BF),...  1.37 us

profile of v6, /device:TPU:2, one launch (start us, length us, event | category | flops | bytes accessed | tf_op | source)
XLA Modules:
  0.0 60.9 jit_solution(9567113455794577997)
XLA Ops:
  0.6 58.9 %key_backward.1 = (bf16[256,4096]{1,0:T(8,128)(2,1)S(1)}, f32[16,512]{1,0:T(8,128)S(1)}) custom-call(bf16[256,4096]{1,0:T(8,128)(2,1)} %tok_hbm.1, bf16[256,4096]{1,0:T(8,128)(2,1)} %q_hbm.1, bf16[256,512]{1,0:T(8,128)(2,1)} %v_hbm.1, bf16[256,4096]{1,0:T(8,128)(2,1)} %u_hbm.1, bf16[16,512]{1,0:T(8,128)(2,1)} %kw_hbm.1, s32[1,256]{1,0:T(1,128)} %bitcast.1), custom_call_target="tpu_custom_call" | custom-call | flops 5000000000 | bytes 9000000 | tf_op jit(solution)/shard_map/key_backward/pallas_call | solution.py:359
  59.5 1.4 %hand_over.1 = (bf16[256,4096]{1,0:T(8,128)(2,1)}, f32[16,512]{1,0:T(8,128)}) custom-call(bf16[256,4096]{1,0:T(8,128)(2,1)S(1)} %get-tuple-element.4.gt, f32[16,512]{1,0:T(8,128)S(1)} %get-tuple-element.5.gw), custom_call_target="tpu_custom_call" | custom-call | tf_op jit(solution)/shard_map/hand_over/pallas_call | solution.py:396
